TPU v7x, 128 devices: a whole 4x4x4 slice. The times are simulated.
128 devices in a mesh: space: 16 (over z, x), tm: 8 (over y, core).
Axes of the slice: x: 4, y: 4, z: 4, core: 2. Of those that a mesh axis runs over, the one named last changes fastest.
Arguments:
- slab: bfloat16 [4096, 128, 1024], P('space', None, 'tm'), may hold values from -22 to 22, as said below
- counts: int32 [4096], replicated, may hold values from 0 to 128
- owner: int32 [4096, 1], replicated, may hold values from 0 to 15; in each aligned block of 256 rows (0 to 255, 256 to 511, ...) at most 24 rows name the same one
- omega: bfloat16 [1024, 128], P('tm'), may hold values from -0.1875 to 0.1875
Outputs:
- probe_owned: bfloat16 [6144, 128, 128], P('space')
- projected: float32 [1024, 128], P('tm')
Inputs may be any that keep to these rules, and one draw needn't show every extreme that they name: Within each aligned block of 256 tiles no owner is named more than 24 times, a bound that some block reaches. `slab`: finite field values.
All inputs are finite; a program needn't handle non-finite values.
Results may differ from a plain program's by a relative error of at most 0.025.
Values may be sent and summed in bfloat16 or wider, within the bound.
A program may use at most 128 MiB of HBM per device.

v0:
```python
import jax
import jax.numpy as jnp
from jax import lax
from jax.sharding import PartitionSpec as P

TIME = 1024


def local(slab, counts, owner, omega):
    spaces = lax.axis_size("space")
    tiles_here, points, block = slab.shape
    limit = max(2, (3 * tiles_here + 2 * spaces - 1) // (2 * spaces))
    start = lax.axis_index("space") * tiles_here
    mine = lax.dynamic_slice_in_dim(counts, start, tiles_here)
    ocean = (jnp.arange(points)[None, :] < mine[:, None]).astype(jnp.float32)
    sums = lax.psum(jnp.sum(slab, axis=2, dtype=jnp.float32).astype(jnp.bfloat16), "tm").astype(
        jnp.float32
    )
    mean = sums / TIME
    anomaly = ((slab.astype(jnp.float32) - mean[..., None]) * ocean[..., None]).astype(jnp.bfloat16)
    targets = lax.dynamic_slice_in_dim(owner[:, 0], start, tiles_here)
    onehot = (targets[:, None] == jnp.arange(spaces)[None, :]).astype(jnp.int32)
    rank = jnp.sum((jnp.cumsum(onehot, axis=0) - onehot) * onehot, axis=1)
    slots = targets * limit + rank
    scale = 1.0 / jnp.sqrt(jnp.sum(counts.astype(jnp.float32)))
    arrived = lax.all_to_all(
        jnp.zeros((spaces * limit,) + anomaly.shape[1:], anomaly.dtype).at[slots].set(anomaly),
        "space",
        split_axis=0,
        concat_axis=0,
        tiled=True,
    )
    term = jnp.einsum("ptc,ck->ptk", arrived, omega, preferred_element_type=jnp.float32)
    rounded = lax.optimization_barrier(term.astype(jnp.bfloat16))
    probe_owned = lax.psum(rounded.astype(jnp.float32).astype(jnp.bfloat16), "tm")
    partial_value = jnp.einsum(
        "ptc,ptk->ck", arrived, probe_owned, preferred_element_type=jnp.float32
    )
    projected = lax.psum(partial_value.astype(jnp.bfloat16), "space").astype(jnp.float32) * scale
    return (probe_owned, projected)


def solution(mesh):
    return jax.shard_map(
        local,
        mesh=mesh,
        in_specs=(P("space", None, "tm"), P(), P(), P("tm", None)),
        out_specs=(P("space", None, None), P("tm", None)),
        check_vma=False,
    )
```

profile of v0, /device:TPU:0, one launch (start us, length us, event | category | flops | bytes accessed | tf_op | source)
XLA Modules:
  0.0 535.7 jit_solution(13094890705031831678)
XLA Ops:
  7.2 6.3 %reduce_sum.34 = bf16[256,128]{1,0:T(8,128)(2,1)} reduce(bf16[256,128,128]{2,1,0:T(8,128)(2,1)} %param.4, bf16[]{:T(256)} %constant.10.clone.1), dimensions={2}, to_apply=%region_3.4 | reduce | flops 4161536 | bytes 8454146 | tf_op jit(solution)/shard_map/reduce_sum | solution.py:16
  13.5 0.0 all-reduce.5.cloned.1.call-start
  13.6 0.7 constant_dynamic-slice_fusion
  14.3 0.6 reduce-window.6
  14.8 0.2 slice_reduce_fusion
  15.1 0.8 dynamic_slice.7
  15.8 0.1 fusion.1
  15.9 0.1 fusion.5
  16.0 0.7 compare_select_fusion
  16.7 58.1 %all-reduce.3.cloned.1.call-done = bf16[256,128]{1,0:T(8,128)(2,1)} async-done(((bf16[256,128]{1,0:T(8,128)(2,1)}), bf16[256,128]{1,0:T(8,128)(2,1)}) %all-reduce.3.cloned.1.call-update) | async-done | bytes 65552 | tf_op jit(solution)/shard_map/psum | solution.py:16
  74.9 0.8 convert_multiply_fusion
  75.7 11.8 %multiply_convert_fusion = bf16[256,128,128]{2,1,0:T(8,128)(2,1)} fusion(bf16[256,128,128]{2,1,0:T(8,128)(2,1)} %param.4, f32[256,128]{1,0:T(8,128)S(1)} %fusion.1, f32[256,128]{1,0:T(8,128)S(1)} %convert_multiply_fusion), kind=kLoop, calls=%fused_computation.1 | loop fusion | flops 16777216 | bytes 17039360 | tf_op jit(solution)/shard_map/convert_element_type | solution.py:20
  87.6 8.0 %broadcast_in_dim.2 = bf16[384,128,128]{2,1,0:T(8,128)(2,1)} broadcast(bf16[]{:T(256)} %constant.10.clone.1), dimensions={} | broadcast | bytes 12582914 | tf_op jit(solution)/shard_map/broadcast_in_dim | solution.py:27
  95.5 36.8 %scatter_fusion = bf16[384,128,128]{2,1,0:T(8,128)(2,1)} fusion(bf16[384,128,128]{2,1,0:T(8,128)(2,1)} %broadcast_in_dim.2, s32[256]{0:T(256)S(1)} %bitcast.35, bf16[256,128,128]{2,1,0:T(8,128)(2,1)} %multiply_convert_fusion), kind=kCustom, calls=%fused_computation | custom fusion | bytes 25166848 | tf_op jit(solution)/shard_map/scatter | solution.py:27
  132.4 146.6 %all_to_all.5 = bf16[384,128,128]{2,1,0:T(8,128)(2,1)S(1)} all-to-all(bf16[384,128,128]{2,1,0:T(8,128)(2,1)} %scatter_fusion), channel_id=1, replica_groups=mesh['space'=16,'tm'=8] {'space'}, dimensions={0} | all-to-all | bytes 25165824 | tf_op jit(solution)/shard_map/all_to_all | solution.py:26
  279.0 4.5 copy-done.2
  283.4 6.6 %convolution_convert_fusion = bf16[384,128,128]{2,1,0:T(8,128)(2,1)} fusion(bf16[384,128,128]{2,1,0:T(8,128)(2,1)S(1)} %all_to_all.5, bf16[128,128]{1,0:T(8,128)(2,1)S(1)} %copy-done), kind=kOutput, calls=%fused_computation.2 | convolution fusion | flops 1616904192 | bytes 25198592 | tf_op jit(solution)/shard_map/ptc,ck->ptk/dot_general | solution.py:33
  290.0 0.7 copy-done.3
  290.7 0.6 convert_reduce_fusion
  292.0 139.4 %all-reduce.5.cloned.1.call-done = bf16[384,128,128]{2,1,0:T(8,128)(2,1)} async-done(((bf16[384,128,128]{2,1,0:T(8,128)(2,1)}), bf16[384,128,128]{2,1,0:T(8,128)(2,1)}) %all-reduce.5.cloned.1.call-update) | async-done | bytes 12582928 | tf_op jit(solution)/shard_map/psum | solution.py:35
  431.4 11.6 %fusion = bf16[128,128]{1,0:T(8,128)(2,1)S(1)} fusion(bf16[384,128,128]{2,1,0:T(8,128)(2,1)} %copy-done.2, bf16[384,128,128]{2,1,0:T(8,128)(2,1)} %all-reduce.5.cloned.1.call-done), kind=kOutput, calls=%fused_computation.4 | convolution fusion | flops 1610629120 | bytes 25198592 | tf_op jit(solution)/shard_map/ptc,ptk->ck/dot_general | solution.py:36
  443.0 74.5 %psum.23 = bf16[128,128]{1,0:T(8,128)(2,1)S(1)} all-reduce(bf16[128,128]{1,0:T(8,128)(2,1)S(1)} %fusion), channel_id=1, replica_groups=mesh['space'=16,'tm'=8] {'space'}, use_global_device_ids=true, to_apply=%region_7.8 | all-reduce | flops 16384 | bytes 65536 | tf_op jit(solution)/shard_map/psum | solution.py:39
  517.5 0.6 convert_multiply_fusion.1
  518.2 10.7 %copy.15 = bf16[384,128,128]{2,1,0:T(8,128)(2,1)} copy(bf16[384,128,128]{2,1,0:T(8,128)(2,1)} %all-reduce.5.cloned.1.call-done) | data formatting | bytes 25165824
  (12 shorter events, 0.1 us)
Async XLA Ops:
  7.2 276.3 %copy-start = (bf16[128,128]{1,0:T(8,128)(2,1)S(1)}, bf16[128,128]{1,0:T(8,128)(2,1)}, u32[]{:S(2)}) copy-start(bf16[128,128]{1,0:T(8,128)(2,1)} %param.7) | copy-start | bytes 98308
  7.2 67.7 %all-reduce.3.cloned.1.call-start = ((), (), s32[]{:S(2)}) async-start(), calls=%async_computation.1 | async-start | bytes 131072 | tf_op jit(solution)/shard_map/psum | solution.py:16
  13.5 417.9 %all-reduce.5.cloned.1.call-start = ((), (), s32[]{:S(2)}) async-start(), calls=%async_computation.2 | async-start | bytes 25165824 | tf_op jit(solution)/shard_map/psum | solution.py:35
  279.0 4.5 copy-start.2
  290.0 0.7 copy-start.3
  517.5 11.4 %copy-start.1 = (bf16[128,128]{1,0:T(8,128)(2,1)S(1)}, bf16[128,128]{1,0:T(8,128)(2,1)}, u32[]{:S(2)}) copy-start(bf16[128,128]{1,0:T(8,128)(2,1)} %param.7) | copy-start | bytes 98308
Sparse Core Ops, SparseCore 0:
  13.6 61.1 all-reduce.2
  290.1 141.1 all-reduce.4
where the time goes:
time: 537 us; the launch traced here: 536 us
  blocking collectives  221 us (41%)
  waiting for transfers between devices  198 us (37%)
  local copies, waits for them, and re-layouts  62.3 us (12%)
  other arithmetic  21.7 us (4%)
  matrix products  18.2 us (3%)
  between operations  14.8 us (3%)
    all_to_all x1, blocking collectives, local(): lax.all_to_all(jnp.zeros((spaces * limit,) + anomaly.shape[1:], anomaly.d...  147 us
    psum x1, waiting for transfers between devices, local(): lax.psum(rounded.astype(jnp.float32).astype(jnp.bfloat16), 'tm')  139 us
    psum x1, blocking collectives, local(): lax.psum(partial_value.astype(jnp.bfloat16), 'space').astype(jnp.float32)  74.5 us
    psum x1, waiting for transfers between devices, local(): lax.psum(jnp.sum(slab, axis=2, dtype=jnp.float32).astype(jnp.bfloat16), '...  58.1 us
    scatter x1, local copies, waits for them, and re-layouts, local(): jnp.zeros((spaces * limit,) + anomaly.shape[1:], anomaly.dtype).at[slots]  36.8 us
    unnamed x9, local copies, waits for them, and re-layouts  15.9 us
    convert_element_type x1, other arithmetic, local(): ((slab.astype(jnp.float32) - mean[..., None]) * ocean[..., None]).astype(...  11.8 us
    dot_general x1, matrix products, local(): jnp.einsum('ptc,ptk->ck', arrived, probe_owned, preferred_element_type=jn...  11.6 us
  transfers between devices with their start and end apart: 2, of which 2 were waited for; matrix products, arithmetic and copies ran while one was open for 1% of the time, Pallas kernels for 0%

commit v1 on v0

v1 whole, which is shorter than its diff:
```python
import functools

import jax
import jax.numpy as jnp
from jax import lax
from jax.experimental import pallas as pl
from jax.experimental.pallas import tpu as pltpu
from jax.sharding import PartitionSpec as P

MESH = pl.DeviceIdType.MESH
BF16 = jnp.bfloat16
F32 = jnp.float32
TIME = 1024
SIDE = 4
SPACES = SIDE * SIDE
TPD = 256
CAP = 24
CLASSES = CAP // 2
PER = -(-TPD // CAP)
PTS = 128
LANES = 128
PIECE = 16
STAGES = 7


def exchange(
    order, cnt, slot, omega, slab_hbm,
    rec, proj,
    slab, swp, swr, omr, rhs, wsend, wrecv, term, rs1, rs2, prb, cur, pack, ph1, ph2, back, vbuf, vrecv, half, ring,
    slab_sem, swap_s, swap_r, small_s, small_r, rs1_s, rs1_r, rs2_s, rs2_r, ag1_s, ag1_r, ag2_s, ag2_r,
    ph1_s, ph1_r, ph2_s, ph2_r, sis_s, sis_r, loc_s,
):
    space, tm = lax.axis_index("space"), lax.axis_index("tm")
    z, x = space // SIDE, space % SIDE
    y, c = tm // 2, tm % 2
    up, down, across = (y + 1) % SIDE, (y + 3) % SIDE, (y + 2) % SIDE
    a = jnp.where(c == 0, x, z)
    b = jnp.where(c == 0, z, x)

    sister = (space, y * 2 + (1 - c))

    def on_y(to):
        return (space, to * 2 + c)

    def on_ab(to_a, to_b):
        to_z = jnp.where(c == 0, to_b, to_a)
        to_x = jnp.where(c == 0, to_a, to_b)
        return (to_z * SIDE + to_x, tm)

    def remote(src, dst, send, recv, to):
        return pltpu.make_async_remote_copy(
            src_ref=src, dst_ref=dst, send_sem=send, recv_sem=recv, device_id=to, device_id_type=MESH
        )

    load = pltpu.make_async_copy(slab_hbm, slab, slab_sem)
    load.start()

    barrier = pltpu.get_barrier_semaphore()
    partners = [sister] + [on_y((y + d) % SIDE) for d in (1, 2, 3)]
    partners += [on_ab((a + d) % SIDE, b) for d in (1, 2, 3)] + [on_ab(a, (b + d) % SIDE) for d in (1, 2, 3)]
    for partner in partners:
        pl.semaphore_signal(barrier, inc=1, device_id=partner, device_id_type=MESH)
    pl.semaphore_wait(barrier, len(partners))

    om_copy = remote(omega, omr, small_s.at[0], small_r.at[0], sister)
    om_copy.start()

    def swap(j):
        return remote(swp.at[j], swr.at[j], swap_s.at[j], swap_r.at[j], sister)

    load.wait()

    @pl.loop(0, CLASSES)
    def _(j):
        @pl.loop(0, PER, unroll=True)
        def _(i):
            swp[j, i] = slab[order[CAP * i + 2 * j + 1 - c]]

        swap(j).start()

    cur[PER] = jnp.zeros((PTS, LANES), BF16)
    back[...] = jnp.zeros_like(back)

    om_copy.wait()
    rhs[:PTS, :LANES] = omega[...]
    rhs[PTS:, :LANES] = omr[...]
    rhs[:, LANES:] = jnp.ones((2 * PTS, LANES), BF16)
    both = omega[...].astype(F32) + omr[...].astype(F32)
    wsend[...] = jnp.broadcast_to(jnp.sum(both, axis=0, keepdims=True), wsend.shape)
    w_copies = [
        remote(wsend, wrecv.at[d - 1], small_s.at[d], small_r.at[d], on_y((y + d) % SIDE)) for d in (1, 2, 3)
    ]
    for copy in w_copies:
        copy.start()
    for copy in w_copies:
        copy.wait()
    wsend[...] = (wsend[...] + wrecv[0] + wrecv[1] + wrecv[2]) * (1.0 / TIME)

    def rs1_copies(j):
        return (
            remote(term.at[j, across, 0], rs1.at[j, 0], rs1_s.at[j, 0], rs1_r.at[j, 0], on_y(up)),
            remote(term.at[j, across, 1], rs1.at[j, 1], rs1_s.at[j, 1], rs1_r.at[j, 1], on_y(down)),
        )

    def rs2_copy(j, k):
        to = up if k < 2 else down
        return remote(term.at[j, to, k % 2], rs2.at[j, k], rs2_s.at[j, k], rs2_r.at[j, k], on_y(to))

    def ag1_copies(j):
        return (
            remote(prb.at[j, y], prb.at[j, y], ag1_s.at[j, 0], ag1_r.at[j, 0], on_y(up)),
            remote(prb.at[j, y], prb.at[j, y], ag1_s.at[j, 1], ag1_r.at[j, 1], on_y(down)),
        )

    def ag2_copies(j):
        return (
            remote(prb.at[j, down, 0], prb.at[j, down, 0], ag2_s.at[j, 0], ag2_r.at[j, 0], on_y(up)),
            remote(prb.at[j, up, 1], prb.at[j, up, 1], ag2_s.at[j, 1], ag2_r.at[j, 1], on_y(down)),
        )

    def ph1_copies(j):
        out = []
        for d in (1, 2, 3):
            to = (a + d) % SIDE
            out.append(
                remote(pack.at[j, to], ph1.at[j, :, a], ph1_s.at[j, d - 1], ph1_r.at[j, d - 1], on_ab(to, b))
            )
        return out

    def ph2_copies(j):
        out = []
        for d in (1, 2, 3):
            to = (b + d) % SIDE
            out.append(remote(ph1.at[j, to], ph2.at[j, b], ph2_s.at[j, d - 1], ph2_r.at[j, d - 1], on_ab(a, to)))
        return out

    def out_copies(j):
        return (
            remote(ph2.at[j], rec.at[c, j], sis_s.at[j], sis_r.at[j], sister),
            pltpu.make_async_copy(ph2.at[j], rec.at[c, j], loc_s.at[j]),
        )

    rows = lax.broadcasted_iota(jnp.int32, (PTS, LANES), 0)

    def terms(j):
        swap(j).wait_recv()
        mean_of = wsend[0:1, :]

        @pl.loop(0, PER, unroll=True)
        def _(i):
            at = CAP * i + 2 * j + c
            both_times = jnp.concatenate([slab[order[at]], swr[j, i]], axis=1)
            acc = jnp.dot(both_times, rhs[...], preferred_element_type=F32)
            value = acc[:, :LANES] - acc[:, LANES:] * mean_of
            value = jnp.where(rows < cnt[at], value, 0.0).astype(BF16)
            for q in range(SIDE):
                for h in range(2):
                    first = (2 * q + h) * PIECE
                    term[j, q, h, i] = value[first : first + PIECE]

        for copy in rs1_copies(j):
            copy.start()
        rs2_copy(j, 1).start()
        rs2_copy(j, 2).start()
        swap(j).wait_send()

    def add_across(j):
        for copy in rs1_copies(j):
            copy.wait_recv()
        term[j, up, 0] = (term[j, up, 0].astype(F32) + rs1[j, 0].astype(F32)).astype(BF16)
        rs2_copy(j, 0).start()
        term[j, down, 1] = (term[j, down, 1].astype(F32) + rs1[j, 1].astype(F32)).astype(BF16)
        rs2_copy(j, 3).start()
        for copy in rs1_copies(j):
            copy.wait_send()

    def finish_sum(j):
        for k in range(4):
            rs2_copy(j, k).wait_recv()
        for h in range(2):
            total = term[j, y, h].astype(F32) + rs2[j, h].astype(F32) + rs2[j, 2 + h].astype(F32)
            prb[j, y, h] = total.astype(BF16)
        for copy in ag1_copies(j):
            copy.start()
        for k in range(4):
            rs2_copy(j, k).wait_send()

    def forward(j):
        for copy in ag1_copies(j):
            copy.wait_recv()
        for copy in ag2_copies(j):
            copy.start()
        for copy in ag1_copies(j):
            copy.wait_send()

    def spread(j):
        for copy in ag2_copies(j):
            copy.wait_recv()

        for i in range(PER):
            for q in range(SIDE):
                for h in range(2):
                    first = (2 * q + h) * PIECE
                    cur[i, first : first + PIECE] = prb[j, q, h, i]

        for to_a in range(SIDE):
            for to_b in range(SIDE):
                pack[j, to_a, to_b] = cur[slot[SPACES * j + SIDE * to_a + to_b]]
        for copy in ph1_copies(j):
            copy.start()
        ph1[j, :, a] = pack[j, a]
        for copy in ag2_copies(j):
            copy.wait_send()

    def project(j):
        def one(i, total):
            both_times = jnp.concatenate([slab[order[CAP * i + 2 * j + c]], swr[j, i]], axis=1)
            return total + lax.dot_general(
                cur[i], both_times, (((0,), (0,)), ((), ())), preferred_element_type=F32
            )

        total = jnp.zeros((LANES, 2 * PTS), F32)
        for i in range(PER):
            total = one(i, total)
        back[...] += total

    def turn(j):
        for copy in ph1_copies(j):
            copy.wait_recv()
        for copy in ph2_copies(j):
            copy.start()
        ph2[j, b] = ph1[j, b]
        for copy in ph1_copies(j):
            copy.wait_send()

    def hand_over(j):
        for copy in ph2_copies(j):
            copy.wait_recv()
        for copy in out_copies(j):
            copy.start()
        for copy in ph2_copies(j):
            copy.wait_send()

    def leave(j):
        sis, loc = out_copies(j)
        sis.wait_send()
        loc.wait()

    def when(t, delay, stage):
        @pl.when((t >= delay) & (t < delay + CLASSES))
        def _():
            stage(t - delay)

    @pl.loop(0, CLASSES + 4)
    def _(t):
        when(t, 0, terms)
        when(t, 4, spread)
        when(t, 4, project)
        when(t, 1, add_across)
        when(t, 2, finish_sum)
        when(t, 3, forward)
        when(t, 5, turn)
        when(t, 6, hand_over)

    last = CLASSES - 1

    v = jnp.sum(back[...], axis=1, keepdims=True)
    vbuf[...] = jnp.broadcast_to(v, vbuf.shape)
    v_copies = [
        remote(vbuf, vrecv.at[d - 1], small_s.at[3 + d], small_r.at[3 + d], on_y((y + d) % SIDE)) for d in (1, 2, 3)
    ]
    for copy in v_copies:
        copy.start()
    hand_over(last - 1)
    turn(last)
    for copy in v_copies:
        copy.wait()
    mean = (vbuf[...] + vrecv[0] + vrecv[1] + vrecv[2]) * (1.0 / TIME)
    half[0] = back[:, :PTS] - mean
    half[1] = back[:, PTS:] - mean
    half_copy = remote(half.at[1], half.at[2], small_s.at[7], small_r.at[7], sister)
    half_copy.start()
    half_copy.wait()
    ring[0, 0] = half[0] + half[2]
    for axis in range(2):
        copies = []
        for d in (1, 2, 3):
            to = on_ab((a + d) % SIDE, b) if axis == 0 else on_ab(a, (b + d) % SIDE)
            copies.append(
                remote(ring.at[axis, 0], ring.at[axis, d], small_s.at[7 + 3 * axis + d], small_r.at[7 + 3 * axis + d], to)
            )
        for copy in copies:
            copy.start()
        if axis == 0:
            hand_over(last)
        for copy in copies:
            copy.wait()
        total = ring[axis, 0] + ring[axis, 1] + ring[axis, 2] + ring[axis, 3]
        if axis == 0:
            ring[1, 0] = total
        else:
            proj[...] = total

    for j in range(CLASSES):
        leave(j)
    for j in range(CLASSES):
        out_copies(j)[0].wait_recv()


def place(table, rec, proj, scale, out, proj_out, sem):
    @pl.loop(0, SPACES * CAP)
    def _(n):
        pltpu.make_async_copy(rec.at[table[n]], out.at[n], sem).start()

    proj_out[...] = proj[...].T * scale[0, 0]
    pltpu.make_async_copy(rec, out, sem).wait()


def local(slab, counts, owner, omega):
    space, tm = lax.axis_index("space"), lax.axis_index("tm")
    c = tm % 2
    names = owner.reshape(SPACES, TPD)
    first = jnp.sum(
        (names[:, None, :] < jnp.arange(SPACES + 1, dtype=jnp.int32)[None, :, None]).astype(jnp.int32), axis=2
    )
    mine = lax.dynamic_index_in_dim(names, space, 0, keepdims=False)
    tiles = jnp.arange(TPD, dtype=jnp.int32)
    key = mine * TPD + tiles
    spot = jnp.sum((key[None, :] < key[:, None]).astype(jnp.int32), axis=1)
    places = jnp.arange(PER * CAP, dtype=jnp.int32)
    hit = spot[None, :] == places[:, None]
    order = jnp.sum(jnp.where(hit, tiles[None, :], 0), axis=1)
    points = lax.dynamic_slice_in_dim(counts, space * TPD, TPD)
    cnt = jnp.sum(jnp.where(hit, points[None, :], 0), axis=1)

    my_first = lax.dynamic_index_in_dim(first, space, 0, keepdims=False)
    begin, end = my_first[:-1], my_first[1:]
    cls = 2 * jnp.arange(CLASSES, dtype=jnp.int32)[:, None] + c
    spot_of = begin[None, :] + (cls - begin[None, :]) % CAP
    slot = jnp.where(spot_of < end[None, :], spot_of // CAP, PER).reshape(CLASSES, SIDE, SIDE)
    slot = jnp.where(c == 0, slot.swapaxes(1, 2), slot).reshape(-1)

    starts = lax.dynamic_index_in_dim(first, space, 1, keepdims=False)
    where = (starts[:, None] + jnp.arange(CAP, dtype=jnp.int32)[None, :]) % CAP
    source = jnp.arange(SPACES, dtype=jnp.int32)[:, None]
    turned = (source % SIDE) * SIDE + source // SIDE
    table = ((where % 2) * CLASSES + where // 2) * SPACES + jnp.where(where % 2 == 0, source, turned)

    scale = 1.0 / jnp.sqrt(jnp.sum(counts.astype(F32)))

    smem, vmem, hbm = (pl.BlockSpec(memory_space=m) for m in (pltpu.SMEM, pltpu.VMEM, pl.ANY))
    dma = pltpu.SemaphoreType.DMA
    piece = (PER, PIECE, LANES)
    tile = (PTS, LANES)
    rec, proj = pl.pallas_call(
        exchange,
        out_shape=(
            jax.ShapeDtypeStruct((2, CLASSES, SIDE, SIDE) + tile, BF16),
            jax.ShapeDtypeStruct(tile, F32),
        ),
        in_specs=[smem, smem, smem, vmem, hbm],
        out_specs=(hbm, vmem),
        scratch_shapes=[
            pltpu.VMEM((TPD,) + tile, BF16),
            pltpu.VMEM((CLASSES, PER) + tile, BF16),
            pltpu.VMEM((CLASSES, PER) + tile, BF16),
            pltpu.VMEM(tile, BF16),
            pltpu.VMEM((2 * PTS, 2 * LANES), BF16),
            pltpu.VMEM((8, LANES), F32),
            pltpu.VMEM((3, 8, LANES), F32),
            pltpu.VMEM((CLASSES, SIDE, 2) + piece, BF16),
            pltpu.VMEM((CLASSES, 2) + piece, BF16),
            pltpu.VMEM((CLASSES, 4) + piece, BF16),
            pltpu.VMEM((CLASSES, SIDE, 2) + piece, BF16),
            pltpu.VMEM((PER + 1,) + tile, BF16),
            pltpu.VMEM((CLASSES, SIDE, SIDE) + tile, BF16),
            pltpu.VMEM((CLASSES, SIDE, SIDE) + tile, BF16),
            pltpu.VMEM((CLASSES, SIDE, SIDE) + tile, BF16),
            pltpu.VMEM((LANES, 2 * PTS), F32),
            pltpu.VMEM((LANES, LANES), F32),
            pltpu.VMEM((3, LANES, LANES), F32),
            pltpu.VMEM((3, LANES, PTS), F32),
            pltpu.VMEM((2, SIDE, LANES, PTS), F32),
            dma,
            dma((CLASSES,)), dma((CLASSES,)),
            dma((14,)), dma((14,)),
            dma((CLASSES, 2)), dma((CLASSES, 2)),
            dma((CLASSES, 4)), dma((CLASSES, 4)),
            dma((CLASSES, 2)), dma((CLASSES, 2)),
            dma((CLASSES, 2)), dma((CLASSES, 2)),
            dma((CLASSES, 3)), dma((CLASSES, 3)),
            dma((CLASSES, 3)), dma((CLASSES, 3)),
            dma((CLASSES,)), dma((CLASSES,)), dma((CLASSES,)),
        ],
        compiler_params=pltpu.CompilerParams(
            collective_id=0, has_side_effects=True, vmem_limit_bytes=60 << 20
        ),
        name="exchange",
    )(order, cnt, slot, omega, slab)
    probe_owned, projected = pl.pallas_call(
        place,
        out_shape=(
            jax.ShapeDtypeStruct((SPACES * CAP,) + tile, BF16),
            jax.ShapeDtypeStruct(tile, F32),
        ),
        in_specs=[smem, hbm, vmem, smem],
        out_specs=(hbm, vmem),
        scratch_shapes=[dma],
        compiler_params=pltpu.CompilerParams(vmem_limit_bytes=16 << 20),
        name="place",
    )(table.reshape(-1), rec.reshape((SPACES * CAP,) + tile), proj, scale.reshape(1, 1))
    return probe_owned, projected


def solution(mesh):
    return jax.shard_map(
        local,
        mesh=mesh,
        in_specs=(P("space", None, "tm"), P(), P(), P("tm", None)),
        out_specs=(P("space", None, None), P("tm", None)),
        check_vma=False,
    )
```

time: 537 us -> 147 us (0.27)
  blocking collectives: 221 us -> 0 us
  waiting for transfers between devices: 198 us -> 0 us
  Pallas kernels: 0 us -> 132 us
  local copies, waits for them, and re-layouts: 62.3 us -> 8.23 us
  matrix products: 18.2 us -> 0 us
  other arithmetic: 21.7 us -> 4.77 us
  between operations: 14.8 us -> 1.47 us
    psum x2 -> x0, waiting for transfers between devices: 198 us -> none  [the longest x1 139 us: local(): lax.psum(rounded.astype(jnp.float32).astype(jnp.bfloat16), 'tm')]
    all_to_all x1 -> x0, blocking collectives: 147 us -> none  [local(): lax.all_to_all(jnp.zeros((spaces * limit,) + anomaly.shape[1:], anomaly.d...]
    pallas_call x0 -> x2, Pallas kernels: none -> 132 us  [the longest x1 126 us: local(): pl.pallas_call(exchange, out_shape=(jax.ShapeDtypeStruct((2, CLASSES, SID...]
    psum x1 -> x0, blocking collectives: 74.5 us -> none  [local(): lax.psum(partial_value.astype(jnp.bfloat16), 'space').astype(jnp.float32)]
    scatter x1 -> x0, local copies, waits for them, and re-layouts: 36.8 us -> none  [local(): jnp.zeros((spaces * limit,) + anomaly.shape[1:], anomaly.dtype).at[slots]]
    dot_general x2 -> x0, matrix products: 18.2 us -> none  [the longest x1 11.6 us: local(): jnp.einsum('ptc,ptk->ck', arrived, probe_owned, preferred_element_type=jn...]
    convert_element_type x3 -> x0, other arithmetic: 12 us -> none  [the longest x1 11.8 us: local(): ((slab.astype(jnp.float32) - mean[..., None]) * ocean[..., None]).astype(...]
    unnamed x9 -> x5, local copies, waits for them, and re-layouts: 15.9 us -> 5.92 us
  transfers between devices with their start and end apart: 2 -> 0, of which waited for: 2 -> 0; matrix products, arithmetic and copies ran while one was open for 1% -> 0% of each run, Pallas kernels for 0% -> 0%
where the time goes in v1:
time: 147 us; the launch traced here: 146 us
  Pallas kernels  132 us (90%)
  local copies, waits for them, and re-layouts  8.23 us (6%)
  other arithmetic  4.77 us (3%)
  between operations  1.47 us (1%)
    pallas_call x1, Pallas kernels, local(): pl.pallas_call(exchange, out_shape=(jax.ShapeDtypeStruct((2, CLASSES, SID...  126 us
    unnamed x5, local copies, waits for them, and re-layouts  5.92 us
    pallas_call x1, Pallas kernels, local(): pl.pallas_call(place, out_shape=(jax.ShapeDtypeStruct((SPACES * CAP,) + t...  5.58 us

profile of v1, /device:TPU:0, one launch (start us, length us, event | category | flops | bytes accessed | tf_op | source)
XLA Modules:
  0.0 146.2 jit_solution(16610103554258926392)
XLA Ops:
  0.6 1.3 convert_reduce_fusion.2
  2.7 0.8 dynamic_slice.17
  3.5 0.1 broadcast_in_dim.59
  3.6 0.1 broadcast_in_dim.57
  3.7 0.5 broadcast.196
  4.2 1.4 reduce.7
  5.7 0.4 convert_reduce_fusion
  6.1 0.2 dynamic-slice_reduce_fusion.1
  6.3 0.2 convert_reduce_fusion.1
  6.4 0.1 add.161
  6.6 0.1 copy.13
  6.7 0.1 copy.12
  6.8 0.8 select_reduce_fusion
  7.7 0.1 rem.97
  7.8 0.1 add.164
  7.9 0.1 lt.115
  8.1 0.1 sub.40
  8.2 0.1 lt.119
  8.4 0.1 add.170
  8.5 0.6 fusion.7.slot
  9.0 126.2 %exchange.1 = (bf16[2,12,4,4,128,128]{5,4,3,2,1,0:T(8,128)(2,1)}, f32[128,128]{1,0:T(8,128)}) custom-call(s32[264]{0:T(512)} %get-tuple-element.9.order, s32[264]{0:T(512)} %get-tuple-element.8.cnt, s32[192]{0:T(256)} %fusion.7.slot, bf16[128,128]{1,0:T(8,128)(2,1)} %omega.1, bf16[256,128,128]{2,1,0:T(8,128)(2,1)} %slab_hbm.1), custom_call_target="tpu_custom_call" | custom-call | tf_op jit(solution)/shard_map/exchange/pallas_call | solution.py:355
  135.2 4.6 %copy-done = bf16[2,12,4,4,128,128]{5,4,3,2,1,0:T(8,128)(2,1)S(1)} copy-done((bf16[2,12,4,4,128,128]{5,4,3,2,1,0:T(8,128)(2,1)S(1)}, bf16[2,12,4,4,128,128]{5,4,3,2,1,0:T(8,128)(2,1)}, u32[]{:S(2)}) %copy-start) | copy-done | bytes 12582936
  139.8 0.8 copy-done.1
  140.6 5.6 %place.1 = (bf16[384,128,128]{2,1,0:T(8,128)(2,1)}, f32[128,128]{1,0:T(8,128)}) custom-call(s32[384]{0:T(512)S(1)} %fusion.2.table, bf16[384,128,128]{2,1,0:T(8,128)(2,1)S(1)} %bitcast.9, f32[128,128]{1,0:T(8,128)S(1)} %copy-done.1, f32[1,1]{1,0:T(1,128)} %bitcast.6.scale), custom_call_target="tpu_custom_call" | custom-call | tf_op jit(solution)/shard_map/place/pallas_call | solution.py:400
  (18 shorter events, 0.4 us)
Async XLA Ops:
  135.2 4.6 %copy-start = (bf16[2,12,4,4,128,128]{5,4,3,2,1,0:T(8,128)(2,1)S(1)}, bf16[2,12,4,4,128,128]{5,4,3,2,1,0:T(8,128)(2,1)}, u32[]{:S(2)}) copy-start(bf16[2,12,4,4,128,128]{5,4,3,2,1,0:T(8,128)(2,1)} %get-tuple-element.4) | copy-start | bytes 37748740
  139.8 0.8 copy-start.1

commit v2 on v1

--- a/solution.py
+++ b/solution.py
@@ -20,15 +20,15 @@
 PTS = 128
 LANES = 128
 PIECE = 16
-STAGES = 7
+DELAYS = (0, 1, 2, 3, 4, 6, 8)
 
 
 def exchange(
     order, cnt, slot, omega, slab_hbm,
     rec, proj,
-    slab, swp, swr, omr, rhs, wsend, wrecv, term, rs1, rs2, prb, cur, pack, ph1, ph2, back, vbuf, vrecv, half, ring,
+    slab, swp, swr, omr, rhs, wsend, wrecv, term, rs1, rs2, prb, cur, pack, ph1, back, vbuf, vrecv, half, ring,
     slab_sem, swap_s, swap_r, small_s, small_r, rs1_s, rs1_r, rs2_s, rs2_r, ag1_s, ag1_r, ag2_s, ag2_r,
-    ph1_s, ph1_r, ph2_s, ph2_r, sis_s, sis_r, loc_s,
+    ph1_s, ph1_r, ph2_s, ph2_r, sis_s, sis_r,
 ):
     space, tm = lax.axis_index("space"), lax.axis_index("tm")
     z, x = space // SIDE, space % SIDE
@@ -131,14 +131,11 @@
         out = []
         for d in (1, 2, 3):
             to = (b + d) % SIDE
-            out.append(remote(ph1.at[j, to], ph2.at[j, b], ph2_s.at[j, d - 1], ph2_r.at[j, d - 1], on_ab(a, to)))
+            out.append(remote(ph1.at[j, to], rec.at[c, j, b], ph2_s.at[j, d - 1], ph2_r.at[j, d - 1], on_ab(a, to)))
         return out
 
-    def out_copies(j):
-        return (
-            remote(ph2.at[j], rec.at[c, j], sis_s.at[j], sis_r.at[j], sister),
-            pltpu.make_async_copy(ph2.at[j], rec.at[c, j], loc_s.at[j]),
-        )
+    def out_copy(j):
+        return remote(rec.at[c, j], rec.at[c, j], sis_s.at[j], sis_r.at[j], sister)
 
     rows = lax.broadcasted_iota(jnp.int32, (PTS, LANES), 0)
 
@@ -229,82 +226,96 @@
             copy.wait_recv()
         for copy in ph2_copies(j):
             copy.start()
-        ph2[j, b] = ph1[j, b]
+        rec[c, j, b] = ph1[j, b]
         for copy in ph1_copies(j):
             copy.wait_send()
 
     def hand_over(j):
         for copy in ph2_copies(j):
             copy.wait_recv()
-        for copy in out_copies(j):
-            copy.start()
+        out_copy(j).start()
         for copy in ph2_copies(j):
             copy.wait_send()
-
-    def leave(j):
-        sis, loc = out_copies(j)
-        sis.wait_send()
-        loc.wait()
 
     def when(t, delay, stage):
         @pl.when((t >= delay) & (t < delay + CLASSES))
         def _():
             stage(t - delay)
 
-    @pl.loop(0, CLASSES + 4)
-    def _(t):
-        when(t, 0, terms)
-        when(t, 4, spread)
-        when(t, 4, project)
-        when(t, 1, add_across)
-        when(t, 2, finish_sum)
-        when(t, 3, forward)
-        when(t, 5, turn)
-        when(t, 6, hand_over)
-
-    last = CLASSES - 1
-
-    v = jnp.sum(back[...], axis=1, keepdims=True)
-    vbuf[...] = jnp.broadcast_to(v, vbuf.shape)
-    v_copies = [
-        remote(vbuf, vrecv.at[d - 1], small_s.at[3 + d], small_r.at[3 + d], on_y((y + d) % SIDE)) for d in (1, 2, 3)
-    ]
-    for copy in v_copies:
-        copy.start()
-    hand_over(last - 1)
-    turn(last)
-    for copy in v_copies:
-        copy.wait()
-    mean = (vbuf[...] + vrecv[0] + vrecv[1] + vrecv[2]) * (1.0 / TIME)
-    half[0] = back[:, :PTS] - mean
-    half[1] = back[:, PTS:] - mean
-    half_copy = remote(half.at[1], half.at[2], small_s.at[7], small_r.at[7], sister)
-    half_copy.start()
-    half_copy.wait()
-    ring[0, 0] = half[0] + half[2]
-    for axis in range(2):
+    def v_copies():
+        return [
+            remote(vbuf, vrecv.at[d - 1], small_s.at[3 + d], small_r.at[3 + d], on_y((y + d) % SIDE))
+            for d in (1, 2, 3)
+        ]
+
+    def half_copy():
+        return remote(half.at[1], half.at[2], small_s.at[7], small_r.at[7], sister)
+
+    def ring_copies(axis):
         copies = []
         for d in (1, 2, 3):
             to = on_ab((a + d) % SIDE, b) if axis == 0 else on_ab(a, (b + d) % SIDE)
-            copies.append(
-                remote(ring.at[axis, 0], ring.at[axis, d], small_s.at[7 + 3 * axis + d], small_r.at[7 + 3 * axis + d], to)
-            )
-        for copy in copies:
-            copy.start()
-        if axis == 0:
-            hand_over(last)
-        for copy in copies:
+            k = 7 + 3 * axis + d
+            copies.append(remote(ring.at[axis, 0], ring.at[axis, d], small_s.at[k], small_r.at[k], to))
+        return copies
+
+    def back_sum():
+        v = jnp.sum(back[...], axis=1, keepdims=True)
+        vbuf[...] = jnp.broadcast_to(v, vbuf.shape)
+        for copy in v_copies():
+            copy.start()
+
+    def back_centre():
+        for copy in v_copies():
             copy.wait()
-        total = ring[axis, 0] + ring[axis, 1] + ring[axis, 2] + ring[axis, 3]
-        if axis == 0:
-            ring[1, 0] = total
-        else:
-            proj[...] = total
+        mean = (vbuf[...] + vrecv[0] + vrecv[1] + vrecv[2]) * (1.0 / TIME)
+        half[0] = back[:, :PTS] - mean
+        half[1] = back[:, PTS:] - mean
+        half_copy().start()
+
+    def back_cores():
+        half_copy().wait()
+        ring[0, 0] = half[0] + half[2]
+        for copy in ring_copies(0):
+            copy.start()
+
+    def back_first():
+        for copy in ring_copies(0):
+            copy.wait()
+        ring[1, 0] = ring[0, 0] + ring[0, 1] + ring[0, 2] + ring[0, 3]
+        for copy in ring_copies(1):
+            copy.start()
+
+    def back_second():
+        for copy in ring_copies(1):
+            copy.wait()
+        proj[...] = ring[1, 0] + ring[1, 1] + ring[1, 2] + ring[1, 3]
+
+    def once(t, at, stage):
+        @pl.when(t == at)
+        def _():
+            stage()
+
+    ended = CLASSES - 1 + DELAYS[4]
+
+    @pl.loop(0, max(CLASSES + DELAYS[6], ended + 5))
+    def _(t):
+        when(t, DELAYS[0], terms)
+        when(t, DELAYS[4], spread)
+        when(t, DELAYS[1], add_across)
+        when(t, DELAYS[2], finish_sum)
+        when(t, DELAYS[3], forward)
+        when(t, DELAYS[5], turn)
+        when(t, DELAYS[6], hand_over)
+        when(t, DELAYS[4], project)
+        once(t, ended, back_sum)
+        once(t, ended + 1, back_centre)
+        once(t, ended + 1, back_cores)
+        once(t, ended + 2, back_first)
+        once(t, ended + 3, back_second)
 
     for j in range(CLASSES):
-        leave(j)
-    for j in range(CLASSES):
-        out_copies(j)[0].wait_recv()
+        out_copy(j).wait()
 
 
 def place(table, rec, proj, scale, out, proj_out, sem):
@@ -355,11 +366,11 @@
     rec, proj = pl.pallas_call(
         exchange,
         out_shape=(
-            jax.ShapeDtypeStruct((2, CLASSES, SIDE, SIDE) + tile, BF16),
+            pltpu.VMEM((2, CLASSES, SIDE, SIDE) + tile, BF16),
             jax.ShapeDtypeStruct(tile, F32),
         ),
         in_specs=[smem, smem, smem, vmem, hbm],
-        out_specs=(hbm, vmem),
+        out_specs=(vmem, vmem),
         scratch_shapes=[
             pltpu.VMEM((TPD,) + tile, BF16),
             pltpu.VMEM((CLASSES, PER) + tile, BF16),
@@ -373,7 +384,6 @@
             pltpu.VMEM((CLASSES, 4) + piece, BF16),
             pltpu.VMEM((CLASSES, SIDE, 2) + piece, BF16),
             pltpu.VMEM((PER + 1,) + tile, BF16),
-            pltpu.VMEM((CLASSES, SIDE, SIDE) + tile, BF16),
             pltpu.VMEM((CLASSES, SIDE, SIDE) + tile, BF16),
             pltpu.VMEM((CLASSES, SIDE, SIDE) + tile, BF16),
             pltpu.VMEM((LANES, 2 * PTS), F32),
@@ -390,10 +400,10 @@
             dma((CLASSES, 2)), dma((CLASSES, 2)),
             dma((CLASSES, 3)), dma((CLASSES, 3)),
             dma((CLASSES, 3)), dma((CLASSES, 3)),
-            dma((CLASSES,)), dma((CLASSES,)), dma((CLASSES,)),
+            dma((CLASSES,)), dma((CLASSES,)),
         ],
         compiler_params=pltpu.CompilerParams(
-            collective_id=0, has_side_effects=True, vmem_limit_bytes=60 << 20
+            collective_id=0, has_side_effects=True, vmem_limit_bytes=46 << 20
         ),
         name="exchange",
     )(order, cnt, slot, omega, slab)

time: 147 us -> 136 us (0.925)
  Pallas kernels: 132 us -> 124 us
  local copies, waits for them, and re-layouts: 8.23 us -> 3.65 us
    pallas_call x1, Pallas kernels: 126 us -> 119 us  [local(): pl.pallas_call(exchange, out_shape=(pltpu.VMEM((2, CLASSES, SIDE, SIDE) +...]
    unnamed x5 -> x3, local copies, waits for them, and re-layouts: 5.92 us -> 1.35 us
where the time goes in v2:
time: 136 us; the launch traced here: 134 us
  Pallas kernels  124 us (91%)
  other arithmetic  4.76 us (4%)
  local copies, waits for them, and re-layouts  3.65 us (3%)
  between operations  1.47 us (1%)
    pallas_call x1, Pallas kernels, local(): pl.pallas_call(exchange, out_shape=(pltpu.VMEM((2, CLASSES, SIDE, SIDE) +...  119 us
    pallas_call x1, Pallas kernels, local(): pl.pallas_call(place, out_shape=(jax.ShapeDtypeStruct((SPACES * CAP,) + t...  5.58 us

profile of v2, /device:TPU:0, one launch (start us, length us, event | category | flops | bytes accessed | tf_op | source)
XLA Modules:
  0.0 134.1 jit_solution(1234882045900161444)
XLA Ops:
  0.6 1.3 convert_reduce_fusion.2
  2.7 0.8 dynamic_slice.17
  3.5 0.1 broadcast_in_dim.59
  3.6 0.1 broadcast_in_dim.57
  3.7 0.5 broadcast.196
  4.2 1.4 %reduce.7 = s32[4096]{0:T(1024)S(1)} reduce(s32[4096,1]{0,1:T(1,128)} %param.6, s32[]{:T(128)} %broadcast.196), dimensions={1}, to_apply=%param.6.reduce_sub_computation.3 | reduce | bytes 32772 | tf_op args[2]
  5.7 0.4 convert_reduce_fusion
  6.1 0.2 dynamic-slice_reduce_fusion.1
  6.3 0.2 convert_reduce_fusion.1
  6.4 0.1 add.161
  6.5 0.1 lt.112
  6.6 0.1 copy.13
  6.7 0.1 copy.12
  6.8 0.8 select_reduce_fusion
  7.7 0.1 rem.97
  7.8 0.1 add.164
  7.9 0.1 lt.115
  8.1 0.1 sub.40
  8.2 0.1 lt.119
  8.4 0.1 add.170
  8.5 0.6 fusion.7.slot
  9.0 118.6 %exchange.1 = (bf16[2,12,4,4,128,128]{5,4,3,2,1,0:T(8,128)(2,1)S(1)}, f32[128,128]{1,0:T(8,128)}) custom-call(s32[264]{0:T(512)} %get-tuple-element.9.order, s32[264]{0:T(512)} %get-tuple-element.8.cnt, s32[192]{0:T(256)} %fusion.7.slot, bf16[128,128]{1,0:T(8,128)(2,1)} %omega.1, bf16[256,128,128]{2,1,0:T(8,128)(2,1)} %slab_hbm.1), custom_call_target="tpu_custom_call" | custom-call | tf_op jit(solution)/shard_map/exchange/pallas_call | solution.py:366
  127.7 0.8 copy-done
  128.5 5.6 %place.1 = (bf16[384,128,128]{2,1,0:T(8,128)(2,1)}, f32[128,128]{1,0:T(8,128)}) custom-call(s32[384]{0:T(512)S(1)} %fusion.2.table, bf16[384,128,128]{2,1,0:T(8,128)(2,1)S(1)} %bitcast.9, f32[128,128]{1,0:T(8,128)S(1)} %copy-done, f32[1,1]{1,0:T(1,128)} %bitcast.6.scale), custom_call_target="tpu_custom_call" | custom-call | tf_op jit(solution)/shard_map/place/pallas_call | solution.py:410
  (16 shorter events, 0.3 us)
Async XLA Ops:
  127.7 0.8 copy-start

commit v3 on v2

--- a/solution.py
+++ b/solution.py
@@ -24,10 +24,10 @@
 
 
 def exchange(
-    order, cnt, slot, omega, slab_hbm,
-    rec, proj,
-    slab, swp, swr, omr, rhs, wsend, wrecv, term, rs1, rs2, prb, cur, pack, ph1, back, vbuf, vrecv, half, ring,
-    slab_sem, swap_s, swap_r, small_s, small_r, rs1_s, rs1_r, rs2_s, rs2_r, ag1_s, ag1_r, ag2_s, ag2_r,
+    names, counts, omega, slab_hbm,
+    rec, proj, info,
+    tab_v, tab, slab, swp, swr, omr, rhs, wsend, wrecv, term, rs1, rs2, prb, cur, pack, ph1, back, vbuf, vrecv, half, ring,
+    tab_sem, slab_sem, swap_s, swap_r, small_s, small_r, rs1_s, rs1_r, rs2_s, rs2_r, ag1_s, ag1_r, ag2_s, ag2_r,
     ph1_s, ph1_r, ph2_s, ph2_r, sis_s, sis_r,
 ):
     space, tm = lax.axis_index("space"), lax.axis_index("tm")
@@ -60,31 +60,46 @@
     partners += [on_ab((a + d) % SIDE, b) for d in (1, 2, 3)] + [on_ab(a, (b + d) % SIDE) for d in (1, 2, 3)]
     for partner in partners:
         pl.semaphore_signal(barrier, inc=1, device_id=partner, device_id_type=MESH)
+
+    lane = lax.broadcasted_iota(jnp.int32, (PTS, LANES), 1)
+    row = lax.broadcasted_iota(jnp.int32, (PTS, LANES), 0)
+    own = [jnp.broadcast_to(names[pl.ds(2 * space + h, 1), :], (PTS, LANES)) for h in range(2)]
+    points = [jnp.broadcast_to(counts[pl.ds(2 * space + h, 1), :], (PTS, LANES)) for h in range(2)]
+    keys = [own[h] * TPD + (lane + LANES * h) for h in range(2)]
+    order_of, begins = [0] * 3, 0
+    for h in range(2):
+        key = keys[h].T
+        before = sum(jnp.where(keys[g] < key, 1, 0) for g in range(2))
+        spot = jnp.sum(before, axis=1, keepdims=True)
+        code = (row + PTS * h) * 256 + points[h].T
+        for g in range(3):
+            hit = jnp.where(spot == lane + LANES * g, code, 0)
+            order_of[g] = order_of[g] + jnp.sum(hit, axis=0, keepdims=True)
+        begins = begins + jnp.sum(jnp.where(own[h].T < lane, 1, 0), axis=0, keepdims=True)
+    for g in range(3):
+        tab_v[:, LANES * g : LANES * (g + 1)] = jnp.broadcast_to(order_of[g], (8, LANES))
+    tab_v[:, 3 * LANES :] = jnp.broadcast_to(begins, (8, LANES))
+    tab_copy = pltpu.make_async_copy(tab_v, tab, tab_sem)
+    tab_copy.start()
+    lower = jnp.where(names[...] < space, 1, 0)
+    info[...] = jnp.broadcast_to(jnp.sum(lower, axis=1, keepdims=True), info.shape)
+
+    def tile_at(place):
+        return jnp.clip(lax.div(tab[0, place], 256), 0, TPD - 1)
+
+    def count_at(place):
+        return lax.rem(tab[0, place], 256)
+
+    def tile_for(j, owner):
+        begin, end = tab[0, 3 * LANES + owner], tab[0, 3 * LANES + 1 + owner]
+        place = begin + lax.rem(2 * j + c + PER * CAP - begin, CAP)
+        return jnp.where(place < end, jnp.clip(lax.div(place, CAP), 0, PER), PER)
+
     pl.semaphore_wait(barrier, len(partners))
 
     om_copy = remote(omega, omr, small_s.at[0], small_r.at[0], sister)
     om_copy.start()
-
-    def swap(j):
-        return remote(swp.at[j], swr.at[j], swap_s.at[j], swap_r.at[j], sister)
-
-    load.wait()
-
-    @pl.loop(0, CLASSES)
-    def _(j):
-        @pl.loop(0, PER, unroll=True)
-        def _(i):
-            swp[j, i] = slab[order[CAP * i + 2 * j + 1 - c]]
-
-        swap(j).start()
-
-    cur[PER] = jnp.zeros((PTS, LANES), BF16)
-    back[...] = jnp.zeros_like(back)
-
     om_copy.wait()
-    rhs[:PTS, :LANES] = omega[...]
-    rhs[PTS:, :LANES] = omr[...]
-    rhs[:, LANES:] = jnp.ones((2 * PTS, LANES), BF16)
     both = omega[...].astype(F32) + omr[...].astype(F32)
     wsend[...] = jnp.broadcast_to(jnp.sum(both, axis=0, keepdims=True), wsend.shape)
     w_copies = [
@@ -92,6 +107,26 @@
     ]
     for copy in w_copies:
         copy.start()
+    rhs[:PTS, :LANES] = omega[...]
+    rhs[PTS:, :LANES] = omr[...]
+    rhs[:, LANES:] = jnp.ones((2 * PTS, LANES), BF16)
+    cur[PER] = jnp.zeros((PTS, LANES), BF16)
+    back[...] = jnp.zeros_like(back)
+
+    def swap(j):
+        return remote(swp.at[j], swr.at[j], swap_s.at[j], swap_r.at[j], sister)
+
+    tab_copy.wait()
+    load.wait()
+
+    @pl.loop(0, CLASSES)
+    def _(j):
+        @pl.loop(0, PER, unroll=True)
+        def _(i):
+            swp[j, i] = slab[tile_at(CAP * i + 2 * j + 1 - c)]
+
+        swap(j).start()
+
     for copy in w_copies:
         copy.wait()
     wsend[...] = (wsend[...] + wrecv[0] + wrecv[1] + wrecv[2]) * (1.0 / TIME)
@@ -146,10 +181,10 @@
         @pl.loop(0, PER, unroll=True)
         def _(i):
             at = CAP * i + 2 * j + c
-            both_times = jnp.concatenate([slab[order[at]], swr[j, i]], axis=1)
+            both_times = jnp.concatenate([slab[tile_at(at)], swr[j, i]], axis=1)
             acc = jnp.dot(both_times, rhs[...], preferred_element_type=F32)
             value = acc[:, :LANES] - acc[:, LANES:] * mean_of
-            value = jnp.where(rows < cnt[at], value, 0.0).astype(BF16)
+            value = jnp.where(rows < count_at(at), value, 0.0).astype(BF16)
             for q in range(SIDE):
                 for h in range(2):
                     first = (2 * q + h) * PIECE
@@ -202,7 +237,8 @@
 
         for to_a in range(SIDE):
             for to_b in range(SIDE):
-                pack[j, to_a, to_b] = cur[slot[SPACES * j + SIDE * to_a + to_b]]
+                owner = jnp.where(c == 0, SIDE * to_b + to_a, SIDE * to_a + to_b)
+                pack[j, to_a, to_b] = cur[tile_for(j, owner)]
         for copy in ph1_copies(j):
             copy.start()
         ph1[j, :, a] = pack[j, a]
@@ -211,7 +247,7 @@
 
     def project(j):
         def one(i, total):
-            both_times = jnp.concatenate([slab[order[CAP * i + 2 * j + c]], swr[j, i]], axis=1)
+            both_times = jnp.concatenate([slab[tile_at(CAP * i + 2 * j + c)], swr[j, i]], axis=1)
             return total + lax.dot_general(
                 cur[i], both_times, (((0,), (0,)), ((), ())), preferred_element_type=F32
             )
@@ -289,7 +325,10 @@
     def back_second():
         for copy in ring_copies(1):
             copy.wait()
-        proj[...] = ring[1, 0] + ring[1, 1] + ring[1, 2] + ring[1, 3]
+        total = ring[1, 0] + ring[1, 1] + ring[1, 2] + ring[1, 3]
+        all_points = jnp.sum(counts[...].astype(F32), axis=0, keepdims=True)
+        scale = 1.0 / jnp.sqrt(jnp.sum(all_points, axis=1, keepdims=True))
+        proj[...] = total.T * scale
 
     def once(t, at, stage):
         @pl.when(t == at)
@@ -318,60 +357,41 @@
         out_copy(j).wait()
 
 
-def place(table, rec, proj, scale, out, proj_out, sem):
-    @pl.loop(0, SPACES * CAP)
-    def _(n):
-        pltpu.make_async_copy(rec.at[table[n]], out.at[n], sem).start()
-
-    proj_out[...] = proj[...].T * scale[0, 0]
+def place(info, rec, proj, out, proj_out, sem):
+    @pl.loop(0, SPACES)
+    def _(source):
+        first = jnp.clip(lax.rem(info[2 * source, 0] + info[2 * source + 1, 0], CAP), 0, CAP - 1)
+        turned = lax.rem(source, SIDE) * SIDE + lax.div(source, SIDE)
+        for r in range(CAP):
+            at = first + r
+            at = jnp.where(at >= CAP, at - CAP, at)
+            odd = lax.rem(at, 2)
+            tile = (odd * CLASSES + lax.div(at, 2)) * SPACES + jnp.where(odd == 0, source, turned)
+            pltpu.make_async_copy(rec.at[tile], out.at[source * CAP + r], sem).start()
+
+    proj_out[...] = proj[...]
     pltpu.make_async_copy(rec, out, sem).wait()
 
 
 def local(slab, counts, owner, omega):
-    space, tm = lax.axis_index("space"), lax.axis_index("tm")
-    c = tm % 2
-    names = owner.reshape(SPACES, TPD)
-    first = jnp.sum(
-        (names[:, None, :] < jnp.arange(SPACES + 1, dtype=jnp.int32)[None, :, None]).astype(jnp.int32), axis=2
-    )
-    mine = lax.dynamic_index_in_dim(names, space, 0, keepdims=False)
-    tiles = jnp.arange(TPD, dtype=jnp.int32)
-    key = mine * TPD + tiles
-    spot = jnp.sum((key[None, :] < key[:, None]).astype(jnp.int32), axis=1)
-    places = jnp.arange(PER * CAP, dtype=jnp.int32)
-    hit = spot[None, :] == places[:, None]
-    order = jnp.sum(jnp.where(hit, tiles[None, :], 0), axis=1)
-    points = lax.dynamic_slice_in_dim(counts, space * TPD, TPD)
-    cnt = jnp.sum(jnp.where(hit, points[None, :], 0), axis=1)
-
-    my_first = lax.dynamic_index_in_dim(first, space, 0, keepdims=False)
-    begin, end = my_first[:-1], my_first[1:]
-    cls = 2 * jnp.arange(CLASSES, dtype=jnp.int32)[:, None] + c
-    spot_of = begin[None, :] + (cls - begin[None, :]) % CAP
-    slot = jnp.where(spot_of < end[None, :], spot_of // CAP, PER).reshape(CLASSES, SIDE, SIDE)
-    slot = jnp.where(c == 0, slot.swapaxes(1, 2), slot).reshape(-1)
-
-    starts = lax.dynamic_index_in_dim(first, space, 1, keepdims=False)
-    where = (starts[:, None] + jnp.arange(CAP, dtype=jnp.int32)[None, :]) % CAP
-    source = jnp.arange(SPACES, dtype=jnp.int32)[:, None]
-    turned = (source % SIDE) * SIDE + source // SIDE
-    table = ((where % 2) * CLASSES + where // 2) * SPACES + jnp.where(where % 2 == 0, source, turned)
-
-    scale = 1.0 / jnp.sqrt(jnp.sum(counts.astype(F32)))
-
+    names = owner.reshape(SPACES * TPD // LANES, LANES)
+    counts = counts.reshape(names.shape)
     smem, vmem, hbm = (pl.BlockSpec(memory_space=m) for m in (pltpu.SMEM, pltpu.VMEM, pl.ANY))
     dma = pltpu.SemaphoreType.DMA
     piece = (PER, PIECE, LANES)
     tile = (PTS, LANES)
-    rec, proj = pl.pallas_call(
+    rec, proj, info = pl.pallas_call(
         exchange,
         out_shape=(
             pltpu.VMEM((2, CLASSES, SIDE, SIDE) + tile, BF16),
             jax.ShapeDtypeStruct(tile, F32),
+            jax.ShapeDtypeStruct(names.shape, jnp.int32),
         ),
-        in_specs=[smem, smem, smem, vmem, hbm],
-        out_specs=(vmem, vmem),
+        in_specs=[vmem, vmem, vmem, hbm],
+        out_specs=(vmem, vmem, vmem),
         scratch_shapes=[
+            pltpu.VMEM((8, 4 * LANES), jnp.int32),
+            pltpu.SMEM((8, 4 * LANES), jnp.int32),
             pltpu.VMEM((TPD,) + tile, BF16),
             pltpu.VMEM((CLASSES, PER) + tile, BF16),
             pltpu.VMEM((CLASSES, PER) + tile, BF16),
@@ -391,7 +411,7 @@
             pltpu.VMEM((3, LANES, LANES), F32),
             pltpu.VMEM((3, LANES, PTS), F32),
             pltpu.VMEM((2, SIDE, LANES, PTS), F32),
-            dma,
+            dma, dma,
             dma((CLASSES,)), dma((CLASSES,)),
             dma((14,)), dma((14,)),
             dma((CLASSES, 2)), dma((CLASSES, 2)),
@@ -406,19 +426,19 @@
             collective_id=0, has_side_effects=True, vmem_limit_bytes=46 << 20
         ),
         name="exchange",
-    )(order, cnt, slot, omega, slab)
+    )(names, counts, omega, slab)
     probe_owned, projected = pl.pallas_call(
         place,
         out_shape=(
             jax.ShapeDtypeStruct((SPACES * CAP,) + tile, BF16),
             jax.ShapeDtypeStruct(tile, F32),
         ),
-        in_specs=[smem, hbm, vmem, smem],
+        in_specs=[smem, hbm, vmem],
         out_specs=(hbm, vmem),
         scratch_shapes=[dma],
         compiler_params=pltpu.CompilerParams(vmem_limit_bytes=16 << 20),
         name="place",
-    )(table.reshape(-1), rec.reshape((SPACES * CAP,) + tile), proj, scale.reshape(1, 1))
+    )(info, rec.reshape((SPACES * CAP,) + tile), proj)
     return probe_owned, projected
 
 

time: 136 us -> 129 us (0.949)
  other arithmetic: 4.76 us -> 0 us
  local copies, waits for them, and re-layouts: 3.65 us -> 1.55 us
  Pallas kernels: 124 us -> 126 us
    reduce_sum x4 -> x0, other arithmetic: 2.66 us -> none  [the longest x1 1.33 us: local(): scale = 1.0 / jnp.sqrt(jnp.sum(counts.astype(F32)))]
    unnamed x1 -> x0, other arithmetic: 1.4 us -> none
where the time goes in v3:
time: 129 us; the launch traced here: 128 us
  Pallas kernels  126 us (98%)
  local copies, waits for them, and re-layouts  1.55 us (1%)
    pallas_call x1, Pallas kernels, local(): pl.pallas_call(exchange, out_shape=(pltpu.VMEM((2, CLASSES, SIDE, SIDE) +...  120 us
    pallas_call x1, Pallas kernels, local(): pl.pallas_call(place, out_shape=(jax.ShapeDtypeStruct((SPACES * CAP,) + t...  5.84 us

profile of v3, /device:TPU:0, one launch (start us, length us, event | category | flops | bytes accessed | tf_op | source)
XLA Modules:
  0.0 127.8 jit_solution(5032537694195719263)
XLA Ops:
  0.6 119.8 %exchange.1 = (bf16[2,12,4,4,128,128]{5,4,3,2,1,0:T(8,128)(2,1)S(1)}, f32[128,128]{1,0:T(8,128)}, s32[32,128]{1,0:T(8,128)}) custom-call(s32[32,128]{1,0:T(8,128)} %bitcast.4, s32[32,128]{1,0:T(8,128)} %bitcast.5, bf16[128,128]{1,0:T(8,128)(2,1)} %omega.1, bf16[256,128,128]{2,1,0:T(8,128)(2,1)} %slab_hbm.1), custom_call_target="tpu_custom_call" | custom-call | tf_op jit(solution)/shard_map/exchange/pallas_call | solution.py:383
  120.4 0.0 copy-start
  120.4 0.8 copy-done
  121.2 0.0 copy-start.1
  121.2 0.7 copy-done.1
  122.0 5.8 %place.1 = (bf16[384,128,128]{2,1,0:T(8,128)(2,1)}, f32[128,128]{1,0:T(8,128)}) custom-call(s32[32,128]{1,0:T(8,128)S(1)} %copy-done.1, bf16[384,128,128]{2,1,0:T(8,128)(2,1)S(1)} %bitcast.3, f32[128,128]{1,0:T(8,128)S(1)} %copy-done), custom_call_target="tpu_custom_call" | custom-call | tf_op jit(solution)/shard_map/place/pallas_call | solution.py:430
Async XLA Ops:
  120.4 0.8 copy-start
  121.2 0.7 copy-start.1
